TPU v7x, 32 devices: a whole 2x2x4 slice. The times are simulated.
32 devices in a mesh: seq: 8 (over z, x), heads: 4 (over y, core).
Axes of the slice: x: 2, y: 2, z: 4, core: 2. Of those that a mesh axis runs over, the one named last changes fastest.
Arguments:
- audio: bfloat16 [2048, 1280], P('seq'), may hold values from -6 to 6
- ln_gain: float32 [1280], replicated, may hold values from 0.25 to 1.75
- ln_shift: float32 [1280], replicated, may hold values from -3 to 3
- enc_wq: bfloat16 [1280, 1024], P(None, 'heads'), may hold values from -0.15625 to 0.15625
- enc_bq: float32 [1024], P('heads'), may hold values from -3 to 3
- enc_wk: bfloat16 [1280, 1024], P(None, 'heads'), may hold values from -4 to 4
- enc_wv: bfloat16 [1280, 1024], P(None, 'heads'), may hold values from -0.15625 to 0.15625
- enc_bv: float32 [1024], P('heads'), may hold values from -3 to 3
- enc_wo: bfloat16 [1024, 1280], P('heads'), may hold values from -0.1875 to 0.1875
- enc_bo: float32 [1280], replicated, may hold values from -3 to 3
- windows: int32 [16], P('heads'), may hold values from 1 to 128, as said below
- dec_wkv: bfloat16 [1280, 8, 256], replicated, may hold values from -4 to 4
- dec_bv: float32 [8, 128], replicated, may hold values from -3 to 3
- text: bfloat16 [4096, 8192], P('seq'), may hold values from -6 to 6
- norm_gain: float32 [8192], replicated, may hold values from 0.25 to 1.75
- dec_wq: bfloat16 [8192, 4096], P('seq', 'heads'), may hold values from -0.0625 to 0.0625
- dec_bq: float32 [4096], P('heads'), may hold values from -3 to 3
- dec_wo: bfloat16 [4096, 8192], P('heads', 'seq'), may hold values from -0.125 to 0.125
- span_start: int32 [4096], P('seq'), may hold values from 0 to 1792, as said below
- span_len: int32 [4096], P('seq'), may hold values from 1 to 256, as said below
Outputs:
- enc_out: bfloat16 [2048, 1280], P(('seq', 'heads'))
- dec_out: bfloat16 [4096, 8192], P('seq', 'heads')
Inputs may be any that keep to these rules, and one draw needn't show every extreme that they name: `windows`: every head's window is 1 to 128; some head has exactly 128 and some head exactly 1. `span_start`: row r's band begins between r * 256 // 512 - 255 and r * 256 // 512, and never before frame 0 or after 2048 - 256; row 0 begins at 0 and the last row at 1792; the last row of every aligned block of 512 rows but the final one begins exactly at r * 256 // 512. `span_len`: row 0 has 256 valid frames and row 1 has one; the last row of every aligned block of 512 rows has 256, unless it is row 1.
All inputs are finite; a program needn't handle non-finite values.
Results may differ from a plain program's by a relative error of at most 0.025.
Values may be sent and summed in bfloat16 or wider, within the bound.
A program may use at most 128 MiB of HBM per device.

v0:
```python
import jax
import jax.numpy as jnp
from jax import lax
from jax.sharding import PartitionSpec as P

EWIN = 128
BAND = 256


def with_halo(block, sides, width):
    for axis, dim in sides:
        count = lax.axis_size(axis)
        forward = [(i, i + 1) for i in range(count - 1)]
        backward = [(target, source) for source, target in forward]
        low = lax.ppermute(
            lax.slice_in_dim(block, block.shape[dim] - width, None, axis=dim), axis, forward
        )
        high = lax.ppermute(lax.slice_in_dim(block, 0, width, axis=dim), axis, backward)
        block = jnp.concatenate([low, block, high], axis=dim)
    return block


def layer_norm(values, gain, shift):
    values = values.astype(jnp.float32)
    centre = values - jnp.mean(values, axis=-1, keepdims=True)
    spread = jnp.mean(centre * centre, axis=-1, keepdims=True)
    return centre * lax.rsqrt(spread + 1e-05) * gain + shift


def rms_norm(values, gain):
    values = values.astype(jnp.float32)
    return values * lax.rsqrt(jnp.mean(values * values, axis=-1, keepdims=True) + 1e-06) * gain


def masked_softmax(scores, valid):
    highest = jnp.max(jnp.where(valid, scores, -jnp.inf), axis=-1, keepdims=True)
    raised = jnp.where(valid, jnp.exp(scores - highest), jnp.zeros_like(scores))
    return (raised / jnp.sum(raised, axis=-1, keepdims=True)).astype(jnp.bfloat16)


def shards(
    audio,
    ln_gain,
    ln_shift,
    enc_wq,
    enc_bq,
    enc_wk,
    enc_wv,
    enc_bv,
    enc_wo,
    enc_bo,
    windows,
    dec_wkv,
    dec_bv,
    text,
    norm_gain,
    dec_wq,
    dec_bq,
    dec_wo,
    span_start,
    span_len,
):
    seq_count = lax.axis_size("seq")
    head_count = lax.axis_size("heads")
    seq_index = lax.axis_index("seq")
    head_index = lax.axis_index("heads")
    frames_dev = audio.shape[0]
    enc_width = audio.shape[1]
    heads_dev = windows.shape[0]
    head_size = enc_wq.shape[1] // heads_dev
    all_frames = frames_dev * seq_count
    hidden = layer_norm(audio, ln_gain, ln_shift).astype(jnp.bfloat16)
    enc_query = (jnp.dot(hidden, enc_wq, preferred_element_type=jnp.float32) + enc_bq).astype(
        jnp.bfloat16
    )
    enc_keys = jnp.dot(hidden, enc_wk, preferred_element_type=jnp.float32).astype(jnp.bfloat16)
    enc_values = (jnp.dot(hidden, enc_wv, preferred_element_type=jnp.float32) + enc_bv).astype(
        jnp.bfloat16
    )
    enc_pairs = jnp.stack([enc_keys, enc_values], axis=1)
    widened = with_halo(enc_pairs, (("seq", 0),), EWIN)
    extent = frames_dev + 2 * EWIN
    key_block = widened[:, 0, :].reshape(extent, heads_dev, head_size)
    value_block = widened[:, 1, :].reshape(extent, heads_dev, head_size)
    query_block = enc_query.reshape(frames_dev, heads_dev, head_size)
    scores = jnp.einsum(
        "qhd,khd->hqk", query_block, key_block, preferred_element_type=jnp.float32
    ) * head_size ** (-0.5)
    row_frames = seq_index * frames_dev + jnp.arange(frames_dev, dtype=jnp.int32)
    col_frames = seq_index * frames_dev - EWIN + jnp.arange(extent, dtype=jnp.int32)
    distance = jnp.abs(row_frames[:, None] - col_frames[None, :])
    inside = (col_frames >= 0) & (col_frames < all_frames)
    valid = (distance[None, :, :] <= windows[:, None, None]) & inside[None, None, :]
    enc_weights = masked_softmax(scores, valid)
    enc_context = jnp.einsum(
        "hqk,khd->qhd", enc_weights, value_block, preferred_element_type=jnp.float32
    )
    enc_context = enc_context.astype(jnp.bfloat16).reshape(frames_dev, heads_dev * head_size)
    enc_term = jnp.dot(enc_context, enc_wo, preferred_element_type=jnp.float32)
    mixed = lax.psum_scatter(
        enc_term.astype(jnp.bfloat16), "heads", scatter_dimension=0, tiled=True
    ).astype(jnp.float32)
    share = frames_dev // head_count
    own_audio = lax.dynamic_slice_in_dim(audio, head_index * share, share, 0)
    enc_out = (own_audio.astype(jnp.float32) + mixed + enc_bo).astype(jnp.bfloat16)
    groups_dev = dec_wkv.shape[1] // head_count
    pair_width = dec_wkv.shape[2]
    dec_head = pair_width // 2
    band_bias = jnp.concatenate([jnp.zeros_like(dec_bv), dec_bv], axis=1)
    frames_all = lax.all_gather(enc_out, "heads", axis=0, tiled=True)
    weight_group = lax.dynamic_slice_in_dim(
        dec_wkv, head_index * groups_dev, groups_dev, 1
    ).reshape(enc_width, groups_dev * pair_width)
    bias_group = lax.dynamic_slice_in_dim(
        band_bias, head_index * groups_dev, groups_dev, 0
    ).reshape(groups_dev * pair_width)
    band_pairs = (
        jnp.dot(frames_all, weight_group, preferred_element_type=jnp.float32) + bias_group
    ).astype(jnp.bfloat16)
    band_pairs = band_pairs.reshape(frames_dev, groups_dev, pair_width)
    band_wide = with_halo(band_pairs, (("seq", 0),), BAND)
    rows_dev = text.shape[0]
    model_width = text.shape[1]
    query_width = dec_wq.shape[1]
    query_heads = query_width // (groups_dev * dec_head)
    normed = rms_norm(text, norm_gain).astype(jnp.bfloat16)
    query_sum = jnp.dot(
        normed,
        lax.all_gather(dec_wq, "seq", axis=0, tiled=True),
        preferred_element_type=jnp.float32,
    )
    dec_query = (
        (query_sum + dec_bq)
        .astype(jnp.bfloat16)
        .reshape(rows_dev, groups_dev, query_heads, dec_head)
    )
    band_extent = band_wide.shape[0]
    band_keys = band_wide[:, :, :dec_head]
    band_values = band_wide[:, :, dec_head:]
    dec_scores = jnp.einsum(
        "rgqd,kgd->rgqk", dec_query, band_keys, preferred_element_type=jnp.float32
    ) * dec_head ** (-0.5)
    band_frames = seq_index * frames_dev - BAND + jnp.arange(band_extent, dtype=jnp.int32)
    in_band = (band_frames[None, :] >= span_start[:, None]) & (
        band_frames[None, :] < (span_start + span_len)[:, None]
    )
    dec_weights = masked_softmax(dec_scores, in_band[:, None, None, :])
    dec_context = jnp.einsum(
        "rgqk,kgd->rgqd", dec_weights, band_values, preferred_element_type=jnp.float32
    )
    dec_context = dec_context.astype(jnp.bfloat16).reshape(rows_dev, query_width)
    dec_term = jnp.dot(
        dec_context,
        lax.all_gather(dec_wo, "seq", axis=1, tiled=True),
        preferred_element_type=jnp.float32,
    )
    summed = lax.psum_scatter(
        dec_term.astype(jnp.bfloat16), "heads", scatter_dimension=1, tiled=True
    ).astype(jnp.float32)
    col_share = model_width // head_count
    own_text = lax.dynamic_slice_in_dim(text, head_index * col_share, col_share, 1)
    dec_out = (own_text.astype(jnp.float32) + summed).astype(jnp.bfloat16)
    return (enc_out, dec_out)


def solution(mesh):
    return jax.shard_map(
        shards,
        mesh=mesh,
        in_specs=(
            P("seq", None),
            P(),
            P(),
            P(None, "heads"),
            P("heads"),
            P(None, "heads"),
            P(None, "heads"),
            P("heads"),
            P("heads", None),
            P(),
            P("heads"),
            P(),
            P(),
            P("seq", None),
            P(),
            P("seq", "heads"),
            P("heads"),
            P("heads", "seq"),
            P("seq"),
            P("seq"),
        ),
        out_specs=(P(("seq", "heads"), None), P("seq", "heads")),
        check_vma=False,
    )
```

profile of v0, /device:TPU:5, one launch (start us, length us, event | category | flops | bytes accessed | tf_op | source)
XLA Modules:
  0.0 592.0 jit_solution(17552323515882099597)
XLA Ops:
  8.1 1.4 convert_reduce_fusion
  9.5 1.4 fusion.28
  10.9 1.8 fusion.35
  13.2 3.1 collective-permute-start
  18.5 3.6 collective-permute-done.1
  22.5 2.8 fusion.61
  25.3 2.1 convolution_convert_fusion.2
  29.9 3.2 constant_dynamic-slice_fusion
  33.1 2.7 copy.44
  35.8 5.4 fusion.2
  41.2 11.6 %reduce-scatter.3.cloned.1.call-done = bf16[64,1280]{1,0:T(8,128)(2,1)} async-done(((bf16[256,1280]{1,0:T(8,128)(2,1)}), bf16[64,1280]{1,0:T(8,128)(2,1)}) %reduce-scatter.3.cloned.1.call-update) | async-done | bytes 163856 | tf_op jit(solution)/shard_map/reduce_scatter | solution.py:100
  53.8 8.5 %all_gather.9 = bf16[256,1280]{1,0:T(8,128)(2,1)S(1)} all-gather(bf16[64,1280]{1,0:T(8,128)(2,1)S(1)} %add_convert_fusion.2), channel_id=1, replica_groups=mesh['seq'=8,'heads'=4] {'heads'}, dimensions={0}, use_global_device_ids=true | all-gather | bytes 819200 | tf_op jit(solution)/shard_map/all_gather | solution.py:110
  62.9 3.1 collective-permute-start.2
  66.5 1.5 collective-permute-start.3
  67.9 4.8 collective-permute-done.2
  74.2 1.7 collective-permute-done.3
  76.6 189.4 %all-gather.3.cloned.1.call-done = bf16[8192,1024]{1,0:T(8,128)(2,1)} async-done(((bf16[1024,1024]{1,0:T(8,128)(2,1)}), bf16[8192,1024]{1,0:T(8,128)(2,1)}) %all-gather.3.cloned.1.call-update) | async-done | bytes 16777232 | tf_op jit(solution)/shard_map/all_gather | solution.py:129
  266.0 14.9 %add_convert_fusion.1 = bf16[512,1024]{1,0:T(8,128)(2,1)S(1)} fusion(bf16[8192,1024]{1,0:T(8,128)(2,1)} %all-gather.3.cloned.1.call-done, bf16[512,8192]{1,0:T(8,128)(2,1)} %param.33, f32[8192]{0:T(1024)S(1)} %copy-done.11, f32[512]{0:T(512)S(1)} %add_rsqrt_fusion, f32[1024]{0:T(1024)S(1)} %copy-done.14), kind=kOutput, calls=%fused_computation.24 | convolution fusion | flops 8607760384 | bytes 26253312 | tf_op jit(solution)/shard_map/dot_general | solution.py:127
  281.6 9.6 %fusion.62 = (f32[512,2,4]{0,2,1:T(4,128)S(1)}, f32[512,2,4,768]{0,3,2,1:T(8,128)}) fusion(pred[512,768]{0,1:T(8,128)(4,1)S(1)} %compare_and_fusion.2, bf16[512,2,4,128]{3,2,1,0:T(4,128)(2,1)S(1)} %reshape.153, bf16[768,2,256]{2,0,1:T(8,128)(2,1)} %constant_dynamic-update-slice_fusion), kind=kOutput, calls=%fused_computation.90 | convolution fusion | flops 1629487872 | bytes 16269312 | tf_op jit(solution)/shard_map/sub | solution.py:37
  291.3 5.9 %fusion.27 = bf16[2,128,512,4]{2,1,3,0:T(8,128)(2,1)S(1)} fusion(f32[512,2,4,768]{0,3,2,1:T(8,128)} %get-tuple-element.9, f32[512,2,4]{0,2,1:T(4,128)S(1)} %get-tuple-element.8, bf16[768,2,256]{2,0,1:T(8,128)(2,1)} %constant_dynamic-update-slice_fusion), kind=kOutput, calls=%fused_computation.37 | convolution fusion | flops 812122112 | bytes 14041088 | tf_op jit(solution)/shard_map/rgqk,kgd->rgqd/dot_general | solution.py:148
  297.2 196.3 %all-gather.5.cloned.1.call-done = bf16[1024,8192]{1,0:T(8,128)(2,1)} async-done(((bf16[1024,1024]{1,0:T(8,128)(2,1)}), bf16[1024,8192]{1,0:T(8,128)(2,1)}) %all-gather.5.cloned.1.call-update) | async-done | bytes 16777232 | tf_op jit(solution)/shard_map/all_gather | solution.py:154
  493.5 16.9 %convolution_convert_fusion = bf16[512,8192]{1,0:T(8,128)(2,1)} fusion(bf16[512,1024]{0,1:T(8,128)(2,1)S(1)} %bitcast.78, bf16[1024,8192]{1,0:T(8,128)(2,1)} %all-gather.5.cloned.1.call-done), kind=kOutput, calls=%fused_computation.12 | convolution fusion | flops 8594128896 | bytes 26214400 | tf_op jit(solution)/shard_map/dot_general | solution.py:152
  510.5 69.6 %reduce-scatter.5.cloned.1.call-done = bf16[512,2048]{1,0:T(8,128)(2,1)} async-done(((bf16[512,8192]{1,0:T(8,128)(2,1)}), bf16[512,2048]{1,0:T(8,128)(2,1)}) %reduce-scatter.5.cloned.1.call-update) | async-done | bytes 2097168 | tf_op jit(solution)/shard_map/reduce_scatter | solution.py:157
  580.1 4.4 add_convert_fusion
  (73 shorter events, 10.3 us)
Async XLA Ops:
  8.0 19.4 %copy-start = (bf16[256,1280]{1,0:T(8,128)(2,1)S(1)}, bf16[256,1280]{1,0:T(8,128)(2,1)}, u32[]{:S(2)}) copy-start(bf16[256,1280]{1,0:T(8,128)(2,1)} %param.28) | copy-start | bytes 1966084
  8.0 4.7 copy-start.2
  8.0 4.7 copy-start.13
  8.0 4.7 copy-start.12
  8.1 4.7 copy-start.9
  8.1 44.8 %reduce-scatter.3.cloned.1.call-start = ((), (), s32[]{:S(2)}) async-start(), calls=%async_computation.2 | async-start | bytes 819200 | tf_op jit(solution)/shard_map/reduce_scatter | solution.py:100
  12.7 5.0 copy-start.10
  12.7 5.0 copy-start.16
  13.2 5.3 collective-permute-start
  16.4 5.7 collective-permute-start.1
  28.6 237.3 %all-gather.3.cloned.1.call-start = ((), (), s32[]{:S(2)}) async-start(), calls=%async_computation.3 | async-start | bytes 18874368 | tf_op jit(solution)/shard_map/all_gather | solution.py:129
  29.2 464.3 %all-gather.5.cloned.1.call-start = ((), (), s32[]{:S(2)}) async-start(), calls=%async_computation.4 | async-start | bytes 18874368 | tf_op jit(solution)/shard_map/all_gather | solution.py:154
  29.8 550.3 %reduce-scatter.5.cloned.1.call-start = ((), (), s32[]{:S(2)}) async-start(), calls=%async_computation.5 | async-start | bytes 10485760 | tf_op jit(solution)/shard_map/reduce_scatter | solution.py:157
  29.9 5.9 %copy-start.7 = (f32[8,128]{1,0:T(8,128)S(1)}, f32[8,128]{1,0:T(8,128)}, u32[]{:S(2)}) copy-start(f32[8,128]{1,0:T(8,128)} %param.32) | copy-start | bytes 12292
  35.8 17.1 %copy-start.5 = (f32[1280]{0:T(1024)S(1)}, f32[1280]{0:T(1024)}, u32[]{:S(2)}) copy-start(f32[1280]{0:T(1024)} %param.29) | copy-start | bytes 15364
  35.8 26.5 %copy-start.3 = (bf16[1280,2,256]{0,2,1:T(8,128)(2,1)S(1)}, bf16[1280,2,256]{0,2,1:T(8,128)(2,1)}, u32[]{:S(2)}) copy-start(bf16[1280,2,256]{0,2,1:T(8,128)(2,1)} %copy.44) | copy-start | bytes 3932164
  41.2 24.8 %copy-start.6 = (s32[512]{0:T(512)S(1)}, s32[512]{0:T(512)}, u32[]{:S(2)}) copy-start(s32[512]{0:T(512)} %param.38) | copy-start | bytes 6148
  41.2 24.8 %copy-start.8 = (s32[512]{0:T(512)S(1)}, s32[512]{0:T(512)}, u32[]{:S(2)}) copy-start(s32[512]{0:T(512)} %param.39) | copy-start | bytes 6148
  53.8 12.6 %copy-start.4 = (bf16[64,1280]{1,0:T(8,128)(2,1)}, bf16[64,1280]{1,0:T(8,128)(2,1)S(1)}, u32[]{:S(2)}) copy-start(bf16[64,1280]{1,0:T(8,128)(2,1)S(1)} %add_convert_fusion.2) | copy-start | bytes 491524
  62.3 203.7 %copy-start.11 = (f32[8192]{0:T(1024)S(1)}, f32[8192]{0:T(1024)}, u32[]{:S(2)}) copy-start(f32[8192]{0:T(1024)} %param.34) | copy-start | bytes 98308
  62.3 203.7 %copy-start.14 = (f32[1024]{0:T(1024)S(1)}, f32[1024]{0:T(1024)}, u32[]{:S(2)}) copy-start(f32[1024]{0:T(1024)} %param.36) | copy-start | bytes 12292
  62.9 9.9 %collective-permute-start.2 = (bf16[256,2,256]{2,0,1:T(8,128)(2,1)S(1)}, bf16[256,2,256]{2,0,1:T(8,128)(2,1)S(1)}, u32[]{:S(2)}, u32[]{:S(2)}) collective-permute-start(bf16[256,2,256]{2,0,1:T(8,128)(2,1)S(1)} %bitcast.72), channel_id=1, source_target_pairs={{0,4},{4,8},{8,12},{12,16},{16,20},{20,24},{24,28},{1,5},{5,9},{9,... | collective-permute-start | bytes 786440 | tf_op jit(solution)/shard_map/ppermute | solution.py:15
  66.5 9.4 %collective-permute-start.3 = (bf16[256,2,256]{2,0,1:T(8,128)(2,1)S(1)}, bf16[256,2,256]{2,0,1:T(8,128)(2,1)S(1)}, u32[]{:S(2)}, u32[]{:S(2)}) collective-permute-start(bf16[256,2,256]{2,0,1:T(8,128)(2,1)S(1)} %bitcast.73), channel_id=1, source_target_pairs={{4,0},{8,4},{12,8},{16,12},{20,16},{24,20},{28,24},{5,1},{9,5},{13... | collective-permute-start | bytes 786440 | tf_op jit(solution)/shard_map/ppermute | solution.py:18
  510.5 74.1 %copy-start.1 = (bf16[256,1280]{1,0:T(8,128)(2,1)S(1)}, bf16[256,1280]{1,0:T(8,128)(2,1)}, u32[]{:S(2)}) copy-start(bf16[256,1280]{1,0:T(8,128)(2,1)} %param.28) | copy-start | bytes 1966084
  (2 other events, 8.8 us)
Sparse Core Ops, SparseCore 0:
  28.8 24.0 reduce-scatter.2
  510.6 69.4 reduce-scatter.4
Sparse Core Ops, SparseCore 1:
  31.2 234.7 all-gather.2
  268.0 225.4 all-gather.4
where the time goes:
time: 595 us; the launch traced here: 592 us
  waiting for transfers between devices  478 us (80%)
  matrix products  56.8 us (10%)
  between operations  15.9 us (3%)
  other arithmetic  14.2 us (2%)
  local copies, waits for them, and re-layouts  9.27 us (2%)
  starting transfers between devices  9.18 us (2%)
  blocking collectives  8.46 us (1%)
    all_gather x1, waiting for transfers between devices, shards(): lax.all_gather(dec_wo, 'seq', axis=1, tiled=True)  196 us
    all_gather x1, waiting for transfers between devices, shards(): lax.all_gather(dec_wq, 'seq', axis=0, tiled=True)  189 us
    reduce_scatter x1, waiting for transfers between devices, shards(): lax.psum_scatter(dec_term.astype(jnp.bfloat16), 'heads', scatter_dimensio...  69.6 us
    dot_general x1, matrix products, shards(): jnp.dot(dec_context, lax.all_gather(dec_wo, 'seq', axis=1, tiled=True), p...  16.9 us
    dot_general x1, matrix products, shards(): jnp.dot(normed, lax.all_gather(dec_wq, 'seq', axis=0, tiled=True), prefer...  14.9 us
    sub x2, matrix products, masked_softmax(): raised = jnp.where(valid, jnp.exp(scores - highest), jnp.zeros_like(scores))  12.4 us
  transfers between devices with their start and end apart: 8, of which 7 were waited for; matrix products, arithmetic and copies ran while one was open for 8% of the time, Pallas kernels for 0%

commit v1 on v0

--- a/solution.py
+++ b/solution.py
@@ -1,6 +1,10 @@
+import functools
+
 import jax
 import jax.numpy as jnp
 from jax import lax
+from jax.experimental import pallas as pl
+from jax.experimental.pallas import tpu as pltpu
 from jax.sharding import PartitionSpec as P
 
 EWIN = 128
@@ -18,6 +22,439 @@
         high = lax.ppermute(lax.slice_in_dim(block, 0, width, axis=dim), axis, backward)
         block = jnp.concatenate([low, block, high], axis=dim)
     return block
+
+
+def shifted(count, offset):
+    return [(i, (i + offset) % count) for i in range(count)]
+
+
+MESH = pl.DeviceIdType.MESH
+TILE = 256
+
+
+def query_kernel(
+    depth_z,
+    depth_x,
+    heads,
+    own_ref,
+    weight_ref,
+    bias_ref,
+    out_ref,
+    rows_all,
+    turned,
+    turned_in,
+    summed,
+    summed_in,
+    total,
+    local_sem,
+    spread_send,
+    rows_recv,
+    share_send,
+    turn_send,
+    turn_recv,
+    sum_send,
+    sum_recv,
+):
+    seq = depth_z * depth_x
+    me = lax.axis_index("seq")
+    head = lax.axis_index("heads")
+    my_z, my_x = me // depth_x, lax.rem(me, depth_x)
+    width = weight_ref.shape[1]
+    tile = min(TILE, width)
+    rows = rows_all.shape[1] * rows_all.shape[2]
+
+    barrier = pltpu.get_barrier_semaphore()
+    for step in range(1, seq):
+        pl.semaphore_signal(
+            barrier, inc=1, device_id=(lax.rem(me + step, seq), head), device_id_type=MESH
+        )
+    for step in range(1, heads):
+        pl.semaphore_signal(
+            barrier, inc=1, device_id=(me, lax.rem(head + step, heads)), device_id_type=MESH
+        )
+    pl.semaphore_wait(barrier, seq - 1 + heads - 1)
+
+    started = []
+
+    def send(source, target, send_sem, recv_sem, device):
+        copy = pltpu.make_async_remote_copy(
+            src_ref=source,
+            dst_ref=target,
+            send_sem=send_sem,
+            recv_sem=recv_sem,
+            device_id=device,
+            device_id_type=MESH,
+        )
+        copy.start()
+        started.append(copy)
+
+    def arrived(target, recv_sem):
+        pltpu.make_async_copy(target, target, recv_sem).wait()
+
+    for step in range(1, seq):
+        goal = lax.rem(me + step, seq)
+        send(
+            own_ref.at[goal],
+            rows_all.at[me, head],
+            spread_send.at[step - 1],
+            rows_recv.at[me, head],
+            (goal, head),
+        )
+    own_copy = pltpu.make_async_copy(own_ref.at[me], rows_all.at[me, head], local_sem)
+    own_copy.start()
+    own_copy.wait()
+    for step in range(seq):
+        source = lax.rem(me + seq - step, seq)
+        if step:
+            arrived(rows_all.at[source, head], rows_recv.at[source, head])
+        for turn in range(1, heads):
+            send(
+                rows_all.at[source, head],
+                rows_all.at[source, head],
+                share_send.at[step, turn - 1],
+                rows_recv.at[source, head],
+                (me, lax.rem(head + turn, heads)),
+            )
+
+    def complete(block):
+        for turn in range(1, heads):
+            other = lax.rem(head + turn, heads)
+            arrived(rows_all.at[block, other], rows_recv.at[block, other])
+
+    def multiply(block, store):
+        values = rows_all.at[block]
+
+        def body(index, carry):
+            columns = pl.ds(pl.multiple_of(index * tile, tile), tile)
+            product = jnp.dot(
+                values[...].reshape(rows, values.shape[2]),
+                weight_ref[:, columns],
+                preferred_element_type=jnp.float32,
+            )
+            store(columns, product)
+            return carry
+
+        lax.fori_loop(0, width // tile, body, 0)
+
+    for i in range(depth_z):
+        goal_z = lax.rem(my_z + depth_z - i, depth_z)
+        for j in range(1, depth_x):
+            goal_x = lax.rem(my_x + depth_x - j, depth_x)
+            block = goal_z * depth_x + goal_x
+            complete(block)
+
+            def keep(columns, product, i=i, j=j):
+                turned[j - 1, i, :, columns] = product.astype(jnp.bfloat16)
+
+            multiply(block, keep)
+            send(
+                turned.at[j - 1, i],
+                turned_in.at[j - 1, i],
+                turn_send.at[j - 1, i],
+                turn_recv.at[j - 1, i],
+                (my_z * depth_x + goal_x, head),
+            )
+
+    for i in [*range(1, depth_z), 0]:
+        goal_z = lax.rem(my_z + depth_z - i, depth_z)
+        block = goal_z * depth_x + my_x
+        complete(block)
+        for j in range(1, depth_x):
+            arrived(turned_in.at[j - 1, i], turn_recv.at[j - 1, i])
+
+        def add(columns, product, i=i):
+            for j in range(1, depth_x):
+                product += turned_in[j - 1, i, :, columns].astype(jnp.float32)
+            if i:
+                summed[i - 1, :, columns] = product.astype(jnp.bfloat16)
+            else:
+                total[:, columns] = product
+
+        multiply(block, add)
+        if i:
+            send(
+                summed.at[i - 1],
+                summed_in.at[i - 1],
+                sum_send.at[i - 1],
+                sum_recv.at[i - 1],
+                (goal_z * depth_x + my_x, head),
+            )
+
+    for i in range(1, depth_z):
+        arrived(summed_in.at[i - 1], sum_recv.at[i - 1])
+
+    def finish(index, carry):
+        columns = pl.ds(pl.multiple_of(index * tile, tile), tile)
+        result = total[:, columns] + bias_ref[:, columns]
+        for i in range(1, depth_z):
+            result += summed_in[i - 1, :, columns].astype(jnp.float32)
+        out_ref[:, columns] = result.astype(jnp.bfloat16)
+        return carry
+
+    lax.fori_loop(0, width // tile, finish, 0)
+    for copy in started:
+        copy.wait_send()
+
+
+def project_queries(own_rows, weight, bias):
+    seq = lax.axis_size("seq")
+    heads = lax.axis_size("heads")
+    depth_z = 4 if seq % 4 == 0 else seq
+    depth_x = seq // depth_z
+    quarter = own_rows.shape[1]
+    depth, width = weight.shape
+    rows = quarter * heads
+    turns = max(depth_x - 1, 1)
+    sums = max(depth_z - 1, 1)
+    vmem = pl.BlockSpec(memory_space=pltpu.VMEM)
+    dma = pltpu.SemaphoreType.DMA
+    return pl.pallas_call(
+        functools.partial(query_kernel, depth_z, depth_x, heads),
+        out_shape=jax.ShapeDtypeStruct((rows, width), jnp.bfloat16),
+        in_specs=[vmem] * 3,
+        out_specs=vmem,
+        scratch_shapes=[
+            pltpu.VMEM((seq, heads, quarter, depth), jnp.bfloat16),
+            pltpu.VMEM((turns, depth_z, rows, width), jnp.bfloat16),
+            pltpu.VMEM((turns, depth_z, rows, width), jnp.bfloat16),
+            pltpu.VMEM((sums, rows, width), jnp.bfloat16),
+            pltpu.VMEM((sums, rows, width), jnp.bfloat16),
+            pltpu.VMEM((rows, width), jnp.float32),
+            dma,
+            dma((seq,)),
+            dma((seq, heads)),
+            dma((seq, heads)),
+            dma((turns, depth_z)),
+            dma((turns, depth_z)),
+            dma((sums,)),
+            dma((sums,)),
+        ],
+        compiler_params=pltpu.CompilerParams(
+            collective_id=0, has_side_effects=True, vmem_limit_bytes=48 * 2**20
+        ),
+        cost_estimate=pl.CostEstimate(
+            flops=2 * rows * seq * depth * width,
+            bytes_accessed=400 * 2**20,
+            transcendentals=0,
+        ),
+    )(own_rows, weight, bias.reshape(1, width))
+
+
+def output_kernel(
+    depth_z,
+    depth_x,
+    heads,
+    own_ref,
+    weight_ref,
+    out_ref,
+    rows_all,
+    terms,
+    terms_in,
+    summed,
+    final_in,
+    local_sem,
+    line_send,
+    turn_send,
+    rows_recv,
+    term_send,
+    term_recv,
+    final_send,
+    final_recv,
+):
+    seq = depth_z * depth_x
+    group = seq // heads
+    me = lax.axis_index("seq")
+    head = lax.axis_index("heads")
+    my_z, my_x = me // depth_x, lax.rem(me, depth_x)
+    owner, slot = me // group, lax.rem(me, group)
+    width = weight_ref.shape[1]
+    tile = min(TILE, width)
+    quarter = summed.shape[1]
+
+    barrier = pltpu.get_barrier_semaphore()
+    for step in range(1, depth_z):
+        goal = lax.rem(my_z + step, depth_z) * depth_x + my_x
+        pl.semaphore_signal(barrier, inc=1, device_id=(goal, head), device_id_type=MESH)
+    for step in range(1, depth_x):
+        goal = my_z * depth_x + lax.rem(my_x + step, depth_x)
+        pl.semaphore_signal(barrier, inc=1, device_id=(goal, head), device_id_type=MESH)
+    for step in range(1, heads):
+        pl.semaphore_signal(
+            barrier, inc=1, device_id=(me, lax.rem(head + step, heads)), device_id_type=MESH
+        )
+    for part in range(group):
+        for other in range(heads):
+            source = head * group + part
+
+            @pl.when(jnp.logical_or(source != me, head != other))
+            def _():
+                pl.semaphore_signal(
+                    barrier, inc=1, device_id=(source, other), device_id_type=MESH
+                )
+
+    self_target = jnp.where(owner == head, 1, 0)
+    pl.semaphore_wait(
+        barrier, depth_z - 1 + depth_x - 1 + heads - 1 + seq - self_target
+    )
+
+    started = []
+
+    def send(source, target, send_sem, recv_sem, device):
+        copy = pltpu.make_async_remote_copy(
+            src_ref=source,
+            dst_ref=target,
+            send_sem=send_sem,
+            recv_sem=recv_sem,
+            device_id=device,
+            device_id_type=MESH,
+        )
+        copy.start()
+        started.append(copy)
+
+    def arrived(target, recv_sem):
+        pltpu.make_async_copy(target, target, recv_sem).wait()
+
+    for step in range(1, depth_z):
+        goal = lax.rem(my_z + step, depth_z) * depth_x + my_x
+        send(own_ref, rows_all.at[me], line_send.at[step - 1], rows_recv.at[me], (goal, head))
+    own_copy = pltpu.make_async_copy(own_ref, rows_all.at[me], local_sem)
+    own_copy.start()
+    own_copy.wait()
+
+    def work(block, place):
+        def body(index, carry):
+            columns = pl.ds(pl.multiple_of(index * tile, tile), tile)
+            terms[block, :, columns] = jnp.dot(
+                rows_all[block], weight_ref[:, columns], preferred_element_type=jnp.float32
+            ).astype(jnp.bfloat16)
+            return carry
+
+        lax.fori_loop(0, width // tile, body, 0)
+        for turn in range(1, heads):
+            other = lax.rem(head + turn, heads)
+            start = pl.multiple_of(other * quarter, quarter)
+            send(
+                terms.at[block, pl.ds(start, quarter)],
+                terms_in.at[turn - 1, block],
+                term_send.at[place, turn - 1],
+                term_recv.at[turn - 1, block],
+                (me, other),
+            )
+
+    def finish(block):
+        start = pl.multiple_of(head * quarter, quarter)
+        result = terms[block, pl.ds(start, quarter)].astype(jnp.float32)
+        for turn in range(1, heads):
+            arrived(terms_in.at[turn - 1, block], term_recv.at[turn - 1, block])
+            result += terms_in[turn - 1, block].astype(jnp.float32)
+        summed[block] = result.astype(jnp.bfloat16)
+        local = jnp.logical_and(block == me, owner == head)
+
+        @pl.when(local)
+        def _():
+            final_in[slot, head] = summed[block]
+
+        @pl.when(jnp.logical_not(local))
+        def _():
+            pltpu.make_async_remote_copy(
+                src_ref=summed.at[block],
+                dst_ref=final_in.at[slot, head],
+                send_sem=final_send.at[block],
+                recv_sem=final_recv.at[slot, head],
+                device_id=(block, owner),
+                device_id_type=MESH,
+            ).start()
+
+    order = [(i, j) for i in range(depth_z) for j in range(depth_x)]
+
+    def block_of(i, j):
+        return lax.rem(my_z + depth_z - i, depth_z) * depth_x + lax.rem(
+            my_x + depth_x - j, depth_x
+        )
+
+    lag = 2 * depth_x
+    for place, (i, j) in enumerate(order):
+        block = block_of(i, j)
+        if j == 0:
+            if i:
+                arrived(rows_all.at[block], rows_recv.at[block])
+            for step in range(1, depth_x):
+                goal = my_z * depth_x + lax.rem(my_x + step, depth_x)
+                send(
+                    rows_all.at[block],
+                    rows_all.at[block],
+                    turn_send.at[i, step - 1],
+                    rows_recv.at[block],
+                    (goal, head),
+                )
+        else:
+            arrived(rows_all.at[block], rows_recv.at[block])
+        work(block, place)
+        if place >= lag:
+            finish(block_of(*order[place - lag]))
+    for pair in order[-lag:]:
+        finish(block_of(*pair))
+    for part in range(group):
+        for other in range(heads):
+            source = head * group + part
+
+            @pl.when(jnp.logical_or(source != me, head != other))
+            def _():
+                arrived(final_in.at[part, other], final_recv.at[part, other])
+
+            out_ref[pl.ds(other * quarter, quarter), pl.ds(part * width, width)] = final_in[
+                part, other
+            ]
+    for copy in started:
+        copy.wait_send()
+    for block in range(seq):
+
+        @pl.when(jnp.logical_not(jnp.logical_and(block == me, owner == head)))
+        def _():
+            arrived(summed.at[block], final_send.at[block])
+
+
+def project_outputs(rows_own, weight):
+    seq = lax.axis_size("seq")
+    heads = lax.axis_size("heads")
+    depth_z = 4 if seq % 4 == 0 else seq
+    depth_x = seq // depth_z
+    group = seq // heads
+    rows, depth = rows_own.shape
+    width = weight.shape[1]
+    quarter = rows // heads
+    turns = max(depth_x - 1, 1)
+    vmem = pl.BlockSpec(memory_space=pltpu.VMEM)
+    dma = pltpu.SemaphoreType.DMA
+    return pl.pallas_call(
+        functools.partial(output_kernel, depth_z, depth_x, heads),
+        out_shape=jax.ShapeDtypeStruct((rows, group * width), jnp.bfloat16),
+        in_specs=[vmem] * 2,
+        out_specs=vmem,
+        scratch_shapes=[
+            pltpu.VMEM((seq, rows, depth), jnp.bfloat16),
+            pltpu.VMEM((seq, rows, width), jnp.bfloat16),
+            pltpu.VMEM((heads - 1, seq, quarter, width), jnp.bfloat16),
+            pltpu.VMEM((seq, quarter, width), jnp.bfloat16),
+            pltpu.VMEM((group, heads, quarter, width), jnp.bfloat16),
+            dma,
+            dma((depth_z,)),
+            dma((depth_z, turns)),
+            dma((seq,)),
+            dma((seq, heads - 1)),
+            dma((heads - 1, seq)),
+            dma((seq,)),
+            dma((group, heads)),
+        ],
+        compiler_params=pltpu.CompilerParams(
+            collective_id=1, has_side_effects=True, vmem_limit_bytes=48 * 2**20
+        ),
+        cost_estimate=pl.CostEstimate(
+            flops=2 * rows * seq * depth * width,
+            bytes_accessed=400 * 2**20,
+            transcendentals=0,
+        ),
+    )(rows_own, weight)
 
 
 def layer_norm(values, gain, shift):
@@ -97,17 +534,28 @@
     )
     enc_context = enc_context.astype(jnp.bfloat16).reshape(frames_dev, heads_dev * head_size)
     enc_term = jnp.dot(enc_context, enc_wo, preferred_element_type=jnp.float32)
-    mixed = lax.psum_scatter(
-        enc_term.astype(jnp.bfloat16), "heads", scatter_dimension=0, tiled=True
-    ).astype(jnp.float32)
     share = frames_dev // head_count
+    pieces = enc_term.astype(jnp.bfloat16).reshape(head_count, share, enc_width)
+    mixed = lax.dynamic_index_in_dim(pieces, head_index, 0, False).astype(jnp.float32)
+    for turn in range(1, head_count):
+        piece = lax.dynamic_index_in_dim(pieces, (head_index + turn) % head_count, 0, False)
+        mixed += lax.ppermute(piece, "heads", shifted(head_count, turn)).astype(jnp.float32)
     own_audio = lax.dynamic_slice_in_dim(audio, head_index * share, share, 0)
     enc_out = (own_audio.astype(jnp.float32) + mixed + enc_bo).astype(jnp.bfloat16)
     groups_dev = dec_wkv.shape[1] // head_count
     pair_width = dec_wkv.shape[2]
     dec_head = pair_width // 2
     band_bias = jnp.concatenate([jnp.zeros_like(dec_bv), dec_bv], axis=1)
-    frames_all = lax.all_gather(enc_out, "heads", axis=0, tiled=True)
+    frames_all = jnp.zeros((head_count, share, enc_width), jnp.bfloat16)
+    frames_all = lax.dynamic_update_index_in_dim(frames_all, enc_out, head_index, 0)
+    for turn in range(1, head_count):
+        frames_all = lax.dynamic_update_index_in_dim(
+            frames_all,
+            lax.ppermute(enc_out, "heads", shifted(head_count, turn)),
+            (head_index + head_count - turn) % head_count,
+            0,
+        )
+    frames_all = frames_all.reshape(frames_dev, enc_width)
     weight_group = lax.dynamic_slice_in_dim(
         dec_wkv, head_index * groups_dev, groups_dev, 1
     ).reshape(enc_width, groups_dev * pair_width)
@@ -123,16 +571,13 @@
     model_width = text.shape[1]
     query_width = dec_wq.shape[1]
     query_heads = query_width // (groups_dev * dec_head)
-    normed = rms_norm(text, norm_gain).astype(jnp.bfloat16)
-    query_sum = jnp.dot(
-        normed,
-        lax.all_gather(dec_wq, "seq", axis=0, tiled=True),
-        preferred_element_type=jnp.float32,
-    )
-    dec_query = (
-        (query_sum + dec_bq)
-        .astype(jnp.bfloat16)
-        .reshape(rows_dev, groups_dev, query_heads, dec_head)
+    quarter = rows_dev // head_count
+    depth = dec_wq.shape[0]
+    own_rows = lax.dynamic_slice_in_dim(text, head_index * quarter, quarter, 0)
+    normed = rms_norm(own_rows, norm_gain).astype(jnp.bfloat16)
+    normed = normed.reshape(quarter, seq_count, depth).transpose(1, 0, 2)
+    dec_query = project_queries(normed, dec_wq, dec_bq).reshape(
+        rows_dev, groups_dev, query_heads, dec_head
     )
     band_extent = band_wide.shape[0]
     band_keys = band_wide[:, :, :dec_head]
@@ -149,14 +594,7 @@
         "rgqk,kgd->rgqd", dec_weights, band_values, preferred_element_type=jnp.float32
     )
     dec_context = dec_context.astype(jnp.bfloat16).reshape(rows_dev, query_width)
-    dec_term = jnp.dot(
-        dec_context,
-        lax.all_gather(dec_wo, "seq", axis=1, tiled=True),
-        preferred_element_type=jnp.float32,
-    )
-    summed = lax.psum_scatter(
-        dec_term.astype(jnp.bfloat16), "heads", scatter_dimension=1, tiled=True
-    ).astype(jnp.float32)
+    summed = project_outputs(dec_context, dec_wo).astype(jnp.float32)
     col_share = model_width // head_count
     own_text = lax.dynamic_slice_in_dim(text, head_index * col_share, col_share, 1)
     dec_out = (own_text.astype(jnp.float32) + summed).astype(jnp.bfloat16)

time: 595 us -> 531 us (0.89)
  waiting for transfers between devices: 478 us -> 9.6 us
  Pallas kernels: 0 us -> 398 us
  starting transfers between devices: 9.18 us -> 52.7 us
  matrix products: 56.8 us -> 25.9 us
  local copies, waits for them, and re-layouts: 9.27 us -> 26.7 us
  between operations: 15.9 us -> 1.22 us
  blocking collectives: 8.46 us -> 0 us
    pallas_call x0 -> x2, Pallas kernels: none -> 398 us  [the longest x1 199 us: project_queries(): pl.pallas_call(functools.partial(query_kernel, depth_z, depth_x, heads),...]
    all_gather x2 -> x0, waiting for transfers between devices: 386 us -> none  [the longest x1 196 us: shards(): lax.all_gather(dec_wo, 'seq', axis=1, tiled=True)]
    reduce_scatter x2 -> x0, waiting for transfers between devices: 81.2 us -> none  [the longest x1 69.6 us: shards(): lax.psum_scatter(dec_term.astype(jnp.bfloat16), 'heads', scatter_dimensio...]
    ppermute x2, starting transfers between devices: 6.25 us -> 45.7 us  [with_halo(): lax.ppermute(lax.slice_in_dim(block, block.shape[dim] - width, None, axis...]
    dot_general x2 -> x0, matrix products: 31.8 us -> none  [the longest x1 16.9 us: shards(): jnp.dot(dec_context, lax.all_gather(dec_wo, 'seq', axis=1, tiled=True), p...]
    all_gather x1 -> x0, blocking collectives: 8.46 us -> none  [shards(): frames_all = lax.all_gather(enc_out, 'heads', axis=0, tiled=True)]
    unnamed x41 -> x56, local copies, waits for them, and re-layouts: 4.21 us -> 10.2 us
  transfers between devices with their start and end apart: 8 -> 10, of which waited for: 7 -> 4; matrix products, arithmetic and copies ran while one was open for 8% -> 5% of each run, Pallas kernels for 0% -> 38%
where the time goes in v1:
time: 531 us
  Pallas kernels  398 us (75%)
  starting transfers between devices  52.7 us (10%)
  local copies, waits for them, and re-layouts  26.7 us (5%)
  matrix products  25.9 us (5%)
  other arithmetic  16.4 us (3%)
  waiting for transfers between devices  9.6 us (2%)
    pallas_call x1, Pallas kernels, project_queries(): pl.pallas_call(functools.partial(query_kernel, depth_z, depth_x, heads),...  199 us
    pallas_call x1, Pallas kernels, project_outputs(): pl.pallas_call(functools.partial(output_kernel, depth_z, depth_x, heads),...  199 us
    ppermute x2, starting transfers between devices, with_halo(): lax.ppermute(lax.slice_in_dim(block, block.shape[dim] - width, None, axis...  45.7 us
    sub x2, matrix products, masked_softmax(): raised = jnp.where(valid, jnp.exp(scores - highest), jnp.zeros_like(scores))  12.3 us
  transfers between devices with their start and end apart: 10, of which 4 were waited for; matrix products, arithmetic and copies ran while one was open for 5% of the time, Pallas kernels for 38%

profile of v1, /device:TPU:5, one launch (start us, length us, event | category | flops | bytes accessed | tf_op | source)
XLA Modules:
  0.0 530.5 jit_solution(2896341611806268711)
XLA Ops:
  0.7 1.4 convert_reduce_fusion
  2.1 1.4 fusion.22
  3.5 1.8 fusion.29
  7.1 3.8 collective-permute-start
  12.2 3.1 constant_dynamic-slice_fusion.1
  15.3 3.2 copy.50
  21.0 4.3 fusion.12
  26.2 2.9 copy.38
  31.1 1.8 copy.32
  32.9 1.8 copy.31
  34.7 4.2 fusion.61
  38.9 2.2 convolution_convert_fusion.1
  44.7 199.1 %shard_map.203 = bf16[512,1024]{1,0:T(8,128)(2,1)S(1)} custom-call(bf16[8,128,1024]{2,1,0:T(8,128)(2,1)S(1)} %bitcast.89, bf16[1024,1024]{1,0:T(8,128)(2,1)S(1)} %copy-done.3, f32[1,1024]{1,0:T(1,128)S(1)} %bitcast.90), custom_call_target="tpu_custom_call" | custom-call | flops 8589934592 | bytes 419430400 | tf_op jit(solution)/shard_map/pallas_call | solution.py:211
  246.5 3.2 constant_dynamic-slice_fusion
  249.7 2.7 copy.49
  254.2 4.5 collective-permute-done.6
  258.8 1.9 fusion.26
  261.4 42.0 %collective-permute-start.8 = (bf16[256,2,256]{2,0,1:T(8,128)(2,1)}, bf16[256,2,256]{2,0,1:T(8,128)(2,1)}, u32[]{:S(2)}, u32[]{:S(2)}) collective-permute-start(bf16[256,2,256]{2,0,1:T(8,128)(2,1)} %bitcast.88), channel_id=1, source_target_pairs={{0,4},{4,8},{8,12},{12,16},{16,20},{20,24},{24,28},{1,5},{5,9},{9,... | collective-permute-start | bytes 786440 | tf_op jit(solution)/shard_map/ppermute | solution.py:19
  307.3 4.6 collective-permute-done.9
  311.9 8.1 %fusion.62 = (f32[512,2,4]{0,2,1:T(4,128)S(1)}, f32[512,2,4,768]{0,3,2,1:T(8,128)}) fusion(pred[512,768]{0,1:T(8,128)(4,1)S(1)} %compare_and_fusion.2, bf16[512,2,4,128]{3,2,1,0:T(4,128)(2,1)S(1)} %reshape.170, bf16[768,2,256]{2,0,1:T(8,128)(2,1)S(1)} %constant_dynamic-update-slice_fusion), kind=kOutput, calls=%fused_computation.98 | convolution fusion | flops 1629487872 | bytes 16269312 | tf_op jit(solution)/shard_map/sub | solution.py:474
  320.0 5.7 %fusion.21 = bf16[2,128,512,4]{2,1,3,0:T(8,128)(2,1)S(1)} fusion(f32[512,2,4,768]{0,3,2,1:T(8,128)} %get-tuple-element.14, f32[512,2,4]{0,2,1:T(4,128)S(1)} %get-tuple-element.13, bf16[768,2,256]{2,0,1:T(8,128)(2,1)S(1)} %constant_dynamic-update-slice_fusion), kind=kOutput, calls=%fused_computation.32 | convolution fusion | flops 812122112 | bytes 14041088 | tf_op jit(solution)/shard_map/rgqk,kgd->rgqd/dot_general | solution.py:593
  326.3 1.6 copy-done.4
  327.9 198.8 %shard_map.204 = bf16[512,2048]{1,0:T(8,128)(2,1)S(1)} custom-call(bf16[512,1024]{1,0:T(8,128)(2,1)S(1)} %copy.48.own_ref, bf16[1024,1024]{1,0:T(8,128)(2,1)S(1)} %copy-done.4), custom_call_target="tpu_custom_call" | custom-call | flops 8589934592 | bytes 419430400 | tf_op jit(solution)/shard_map/pallas_call | solution.py:429
  526.7 3.8 add_convert_fusion
  (96 shorter events, 21.5 us)
Async XLA Ops:
  0.6 40.5 %copy-start = (bf16[256,1280]{1,0:T(8,128)(2,1)S(1)}, bf16[256,1280]{1,0:T(8,128)(2,1)}, u32[]{:S(2)}) copy-start(bf16[256,1280]{1,0:T(8,128)(2,1)} %param.28) | copy-start | bytes 1966084
  0.6 4.6 copy-start.6
  0.7 4.6 copy-start.17
  0.7 4.6 copy-start.19
  0.7 4.6 copy-start.21
  0.7 4.6 copy-start.15
  7.1 22.0 %collective-permute-start = (bf16[128,2,256]{2,0,1:T(8,128)(2,1)}, bf16[128,2,256]{2,0,1:T(8,128)(2,1)}, u32[]{:S(2)}, u32[]{:S(2)}) collective-permute-start(bf16[128,2,256]{2,0,1:T(8,128)(2,1)} %get-tuple-element.9), channel_id=1, source_target_pairs={{0,4},{4,8},{8,12},{12,16},{16,20},{20,24},{24,28},{1,5},{5,9},{9,... | collective-permute-start | bytes 393224 | tf_op jit(solution)/shard_map/ppermute | solution.py:19
  10.9 18.3 %collective-permute-start.1 = (bf16[128,2,256]{2,0,1:T(8,128)(2,1)}, bf16[128,2,256]{2,0,1:T(8,128)(2,1)}, u32[]{:S(2)}, u32[]{:S(2)}) collective-permute-start(bf16[128,2,256]{2,0,1:T(8,128)(2,1)} %get-tuple-element.10), channel_id=1, source_target_pairs={{4,0},{8,4},{12,8},{16,12},{20,16},{24,20},{28,24},{5,1},{9,5},{13... | collective-permute-start | bytes 393224 | tf_op jit(solution)/shard_map/ppermute | solution.py:22
  29.1 5.6 %copy-start.23 = (s32[4]{0:T(128)S(1)}, s32[4]{0:T(128)}, u32[]{:S(2)}) copy-start(s32[4]{0:T(128)} %param.30) | copy-start | bytes 52
  30.2 4.4 copy-start.24
  42.3 202.5 %collective-permute-start.2 = (bf16[64,1280]{1,0:T(8,128)(2,1)}, bf16[64,1280]{1,0:T(8,128)(2,1)}, u32[]{:S(2)}, u32[]{:S(2)}) collective-permute-start(bf16[64,1280]{1,0:T(8,128)(2,1)} %get-tuple-element.4), channel_id=1, source_target_pairs={{0,1},{1,2},{2,3},{3,0},{4,5},{5,6},{6,7},{7,4},{8,9},{9,10},{10,1... | collective-permute-start | bytes 491528 | tf_op jit(solution)/shard_map/ppermute | solution.py:542
  43.4 201.4 %collective-permute-start.4 = (bf16[64,1280]{1,0:T(8,128)(2,1)}, bf16[64,1280]{1,0:T(8,128)(2,1)}, u32[]{:S(2)}, u32[]{:S(2)}) collective-permute-start(bf16[64,1280]{1,0:T(8,128)(2,1)} %get-tuple-element.5), channel_id=1, source_target_pairs={{0,3},{1,0},{2,1},{3,2},{4,7},{5,4},{6,5},{7,6},{8,11},{9,8},{10,9... | collective-permute-start | bytes 491528 | tf_op jit(solution)/shard_map/ppermute | solution.py:542
  43.4 201.4 %collective-permute-start.3 = (bf16[64,1280]{1,0:T(8,128)(2,1)}, bf16[64,1280]{1,0:T(8,128)(2,1)}, u32[]{:S(2)}, u32[]{:S(2)}) collective-permute-start(bf16[64,1280]{1,0:T(8,128)(2,1)} %get-tuple-element.6), channel_id=1, source_target_pairs={{0,2},{1,3},{2,0},{3,1},{4,6},{5,7},{6,4},{7,5},{8,10},{9,11},{10,... | collective-permute-start | bytes 491528 | tf_op jit(solution)/shard_map/ppermute | solution.py:542
  44.7 200.2 %copy-start.11 = (f32[1280]{0:T(1024)S(1)}, f32[1280]{0:T(1024)}, u32[]{:S(2)}) copy-start(f32[1280]{0:T(1024)} %param.29) | copy-start | bytes 15364
  44.7 201.8 %copy-start.13 = (f32[8,128]{1,0:T(8,128)S(1)}, f32[8,128]{1,0:T(8,128)}, u32[]{:S(2)}) copy-start(f32[8,128]{1,0:T(8,128)} %param.32) | copy-start | bytes 12292
  246.2 6.7 %copy-start.9 = (bf16[64,1280]{1,0:T(8,128)(2,1)}, bf16[64,1280]{1,0:T(8,128)(2,1)S(1)}, u32[]{:S(2)}) copy-start(bf16[64,1280]{1,0:T(8,128)(2,1)S(1)} %get-tuple-element.3) | copy-start | bytes 491524
  246.2 8.0 %collective-permute-start.5 = (bf16[64,1280]{1,0:T(8,128)(2,1)S(1)}, bf16[64,1280]{1,0:T(8,128)(2,1)S(1)}, u32[]{:S(2)}, u32[]{:S(2)}) collective-permute-start(bf16[64,1280]{1,0:T(8,128)(2,1)S(1)} %get-tuple-element.3), channel_id=1, source_target_pairs={{0,1},{1,2},{2,3},{3,0},{4,5},{5,6},{6,7},{7,4},{8,9},{9,10},{10,1... | collective-permute-start | bytes 491528 | tf_op jit(solution)/shard_map/ppermute | solution.py:554
  252.4 51.0 %copy-start.2 = (bf16[512,1024]{1,0:T(8,128)(2,1)S(1)}, bf16[512,1024]{1,0:T(8,128)(2,1)}, u32[]{:S(2)}) copy-start(bf16[512,1024]{1,0:T(8,128)(2,1)} %copy-done.1) | copy-start | bytes 3145732
  252.4 6.4 %collective-permute-start.7 = (bf16[64,1280]{1,0:T(8,128)(2,1)S(1)}, bf16[64,1280]{1,0:T(8,128)(2,1)S(1)}, u32[]{:S(2)}, u32[]{:S(2)}) collective-permute-start(bf16[64,1280]{1,0:T(8,128)(2,1)S(1)} %get-tuple-element.3), channel_id=1, source_target_pairs={{0,3},{1,0},{2,1},{3,2},{4,7},{5,4},{6,5},{7,6},{8,11},{9,8},{10,9... | collective-permute-start | bytes 491528 | tf_op jit(solution)/shard_map/ppermute | solution.py:554
  252.9 5.8 %collective-permute-start.6 = (bf16[64,1280]{1,0:T(8,128)(2,1)S(1)}, bf16[64,1280]{1,0:T(8,128)(2,1)S(1)}, u32[]{:S(2)}, u32[]{:S(2)}) collective-permute-start(bf16[64,1280]{1,0:T(8,128)(2,1)S(1)} %get-tuple-element.3), channel_id=1, source_target_pairs={{0,2},{1,3},{2,0},{3,1},{4,6},{5,7},{6,4},{7,5},{8,10},{9,11},{10,... | collective-permute-start | bytes 491528 | tf_op jit(solution)/shard_map/ppermute | solution.py:554
  258.8 45.3 %copy-start.12 = (s32[512]{0:T(512)S(1)}, s32[512]{0:T(512)}, u32[]{:S(2)}) copy-start(s32[512]{0:T(512)} %param.38) | copy-start | bytes 6148
  258.8 45.3 %copy-start.14 = (s32[512]{0:T(512)S(1)}, s32[512]{0:T(512)}, u32[]{:S(2)}) copy-start(s32[512]{0:T(512)} %param.39) | copy-start | bytes 6148
  261.4 44.9 %collective-permute-start.8 = (bf16[256,2,256]{2,0,1:T(8,128)(2,1)}, bf16[256,2,256]{2,0,1:T(8,128)(2,1)}, u32[]{:S(2)}, u32[]{:S(2)}) collective-permute-start(bf16[256,2,256]{2,0,1:T(8,128)(2,1)} %bitcast.88), channel_id=1, source_target_pairs={{0,4},{4,8},{8,12},{12,16},{16,20},{20,24},{24,28},{1,5},{5,9},{9,... | collective-permute-start | bytes 786440 | tf_op jit(solution)/shard_map/ppermute | solution.py:19
  304.6 7.3 %collective-permute-start.9 = (bf16[256,2,256]{2,0,1:T(8,128)(2,1)}, bf16[256,2,256]{2,0,1:T(8,128)(2,1)S(1)}, u32[]{:S(2)}, u32[]{:S(2)}) collective-permute-start(bf16[256,2,256]{2,0,1:T(8,128)(2,1)} %bitcast.88), channel_id=1, source_target_pairs={{4,0},{8,4},{12,8},{16,12},{20,16},{24,20},{28,24},{5,1},{9,5},{13... | collective-permute-start | bytes 786440 | tf_op jit(solution)/shard_map/ppermute | solution.py:22
  (11 other events, 20.5 us)

commit v2 on v1

--- a/solution.py
+++ b/solution.py
@@ -576,6 +576,7 @@
     own_rows = lax.dynamic_slice_in_dim(text, head_index * quarter, quarter, 0)
     normed = rms_norm(own_rows, norm_gain).astype(jnp.bfloat16)
     normed = normed.reshape(quarter, seq_count, depth).transpose(1, 0, 2)
+    normed, band_wide = lax.optimization_barrier((normed, band_wide))
     dec_query = project_queries(normed, dec_wq, dec_bq).reshape(
         rows_dev, groups_dev, query_heads, dec_head
     )

time: 531 us -> 540 us (1.017)
  starting transfers between devices: 52.7 us -> 16.9 us
  Pallas kernels: 398 us -> 432 us
    pallas_call x1, Pallas kernels: 199 us -> 238 us  [project_outputs(): pl.pallas_call(functools.partial(output_kernel, depth_z, depth_x, heads),...]
    ppermute x2, starting transfers between devices: 45.7 us -> 9.37 us  [with_halo(): lax.ppermute(lax.slice_in_dim(block, block.shape[dim] - width, None, axis...]
  transfers between devices with their start and end apart: 10 -> 10, of which waited for: 4 -> 5; matrix products, arithmetic and copies ran while one was open for 5% -> 4% of each run, Pallas kernels for 38% -> 0%
where the time goes in v2:
time: 540 us; the launch traced here: 538 us
  Pallas kernels  432 us (80%)
  local copies, waits for them, and re-layouts  28.7 us (5%)
  matrix products  26.1 us (5%)
  other arithmetic  19.1 us (4%)
  starting transfers between devices  16.9 us (3%)
  waiting for transfers between devices  13.9 us (3%)
    pallas_call x1, Pallas kernels, project_outputs(): pl.pallas_call(functools.partial(output_kernel, depth_z, depth_x, heads),...  238 us
    pallas_call x1, Pallas kernels, project_queries(): pl.pallas_call(functools.partial(query_kernel, depth_z, depth_x, heads),...  194 us
    sub x2, matrix products, masked_softmax(): raised = jnp.where(valid, jnp.exp(scores - highest), jnp.zeros_like(scores))  12.4 us
    unnamed x56, local copies, waits for them, and re-layouts  11.7 us
  transfers between devices with their start and end apart: 10, of which 5 were waited for; matrix products, arithmetic and copies ran while one was open for 4% of the time, Pallas kernels for 0%

profile of v2, /device:TPU:5, one launch (start us, length us, event | category | flops | bytes accessed | tf_op | source)
XLA Modules:
  0.0 538.1 jit_solution(14855930403941823330)
XLA Ops:
  3.5 1.8 fusion.29
  7.1 3.8 collective-permute-start
  12.2 3.1 constant_dynamic-slice_fusion.1
  15.3 3.2 copy.49
  23.8 1.8 copy.32
  25.6 1.8 copy.31
  27.4 4.3 fusion.71
  31.7 2.2 convolution_convert_fusion.1
  38.3 4.3 fusion.12
  43.8 2.3 collective-permute-done.3
  48.8 3.2 constant_dynamic-slice_fusion
  52.0 2.7 copy.50
  56.1 4.2 collective-permute-done.6
  60.7 1.8 fusion.26
  63.9 5.6 %collective-permute-start.8 = (bf16[256,2,256]{2,0,1:T(8,128)(2,1)S(1)}, bf16[256,2,256]{2,0,1:T(8,128)(2,1)}, u32[]{:S(2)}, u32[]{:S(2)}) collective-permute-start(bf16[256,2,256]{2,0,1:T(8,128)(2,1)S(1)} %bitcast.96), channel_id=1, source_target_pairs={{0,4},{4,8},{8,12},{12,16},{16,20},{20,24},{24,28},{1,5},{5,9},{9,... | collective-permute-start | bytes 786440 | tf_op jit(solution)/shard_map/ppermute | solution.py:19
  69.6 2.9 copy.34
  73.6 5.7 %collective-permute-done.8 = bf16[256,2,256]{2,0,1:T(8,128)(2,1)} collective-permute-done((bf16[256,2,256]{2,0,1:T(8,128)(2,1)S(1)}, bf16[256,2,256]{2,0,1:T(8,128)(2,1)}, u32[]{:S(2)}, u32[]{:S(2)}) %collective-permute-start.8) | collective-permute-done | bytes 262176 | tf_op jit(solution)/shard_map/ppermute | solution.py:19
  79.4 1.9 pad_maximum_fusion
  82.9 194.2 %shard_map.203 = bf16[512,1024]{1,0:T(8,128)(2,1)S(1)} custom-call(bf16[8,128,1024]{2,1,0:T(8,128)(2,1)S(1)} %bitcast.88, bf16[1024,1024]{1,0:T(8,128)(2,1)S(1)} %copy-done.2, f32[1,1024]{1,0:T(1,128)S(1)} %bitcast.89), custom_call_target="tpu_custom_call" | custom-call | flops 8589934592 | bytes 419430400 | tf_op jit(solution)/shard_map/pallas_call | solution.py:211
  278.1 1.9 reshape.170
  280.0 8.1 %fusion.72 = (f32[512,2,4]{0,2,1:T(4,128)S(1)}, f32[512,2,4,768]{0,3,2,1:T(8,128)}) fusion(pred[512,768]{0,1:T(8,128)(4,1)S(1)} %copy-done.9, bf16[512,2,4,128]{3,2,1,0:T(4,128)(2,1)S(1)} %reshape.170, bf16[768,2,256]{2,0,1:T(8,128)(2,1)S(1)} %copy-done.7), kind=kOutput, calls=%fused_computation.100 | convolution fusion | flops 1629487872 | bytes 16269312 | tf_op jit(solution)/shard_map/sub | solution.py:474
  288.1 5.9 %fusion.21 = bf16[2,128,512,4]{2,1,3,0:T(8,128)(2,1)S(1)} fusion(f32[512,2,4,768]{0,3,2,1:T(8,128)} %get-tuple-element.18, f32[512,2,4]{0,2,1:T(4,128)S(1)} %get-tuple-element.17, bf16[768,2,256]{2,0,1:T(8,128)(2,1)} %pad_maximum_fusion), kind=kOutput, calls=%fused_computation.32 | convolution fusion | flops 812122112 | bytes 14041088 | tf_op jit(solution)/shard_map/rgqk,kgd->rgqd/dot_general | solution.py:594
  296.1 238.2 %shard_map.204 = bf16[512,2048]{1,0:T(8,128)(2,1)S(1)} custom-call(bf16[512,1024]{1,0:T(8,128)(2,1)S(1)} %copy.48.own_ref, bf16[1024,1024]{1,0:T(8,128)(2,1)S(1)} %copy-done.3), custom_call_target="tpu_custom_call" | custom-call | flops 8589934592 | bytes 419430400 | tf_op jit(solution)/shard_map/pallas_call | solution.py:429
  534.3 3.8 add_convert_fusion
  (96 shorter events, 28.3 us)
Async XLA Ops:
  0.6 33.3 %copy-start = (bf16[256,1280]{1,0:T(8,128)(2,1)S(1)}, bf16[256,1280]{1,0:T(8,128)(2,1)}, u32[]{:S(2)}) copy-start(bf16[256,1280]{1,0:T(8,128)(2,1)} %param.28) | copy-start | bytes 1966084
  0.6 4.6 copy-start.5
  0.7 4.6 copy-start.18
  0.7 4.6 copy-start.20
  0.7 4.6 copy-start.22
  0.7 4.6 copy-start.16
  7.1 14.8 %collective-permute-start = (bf16[128,2,256]{2,0,1:T(8,128)(2,1)}, bf16[128,2,256]{2,0,1:T(8,128)(2,1)}, u32[]{:S(2)}, u32[]{:S(2)}) collective-permute-start(bf16[128,2,256]{2,0,1:T(8,128)(2,1)} %get-tuple-element.13), channel_id=1, source_target_pairs={{0,4},{4,8},{8,12},{12,16},{16,20},{20,24},{24,28},{1,5},{5,9},{9,... | collective-permute-start | bytes 393224 | tf_op jit(solution)/shard_map/ppermute | solution.py:19
  10.9 11.0 %collective-permute-start.1 = (bf16[128,2,256]{2,0,1:T(8,128)(2,1)}, bf16[128,2,256]{2,0,1:T(8,128)(2,1)}, u32[]{:S(2)}, u32[]{:S(2)}) collective-permute-start(bf16[128,2,256]{2,0,1:T(8,128)(2,1)} %get-tuple-element.14), channel_id=1, source_target_pairs={{4,0},{8,4},{12,8},{16,12},{20,16},{24,20},{28,24},{5,1},{9,5},{13... | collective-permute-start | bytes 393224 | tf_op jit(solution)/shard_map/ppermute | solution.py:22
  20.9 6.5 %copy-start.24 = (s32[4]{0:T(128)S(1)}, s32[4]{0:T(128)}, u32[]{:S(2)}) copy-start(s32[4]{0:T(128)} %param.30) | copy-start | bytes 52
  23.0 4.4 copy-start.25
  33.9 4.4 copy-start.11
  36.0 6.7 %collective-permute-start.2 = (bf16[64,1280]{1,0:T(8,128)(2,1)}, bf16[64,1280]{1,0:T(8,128)(2,1)}, u32[]{:S(2)}, u32[]{:S(2)}) collective-permute-start(bf16[64,1280]{1,0:T(8,128)(2,1)} %get-tuple-element.8), channel_id=1, source_target_pairs={{0,1},{1,2},{2,3},{3,0},{4,5},{5,6},{6,7},{7,4},{8,9},{9,10},{10,1... | collective-permute-start | bytes 491528 | tf_op jit(solution)/shard_map/ppermute | solution.py:542
  37.0 6.8 %collective-permute-start.4 = (bf16[64,1280]{1,0:T(8,128)(2,1)}, bf16[64,1280]{1,0:T(8,128)(2,1)}, u32[]{:S(2)}, u32[]{:S(2)}) collective-permute-start(bf16[64,1280]{1,0:T(8,128)(2,1)} %get-tuple-element.9), channel_id=1, source_target_pairs={{0,3},{1,0},{2,1},{3,2},{4,7},{5,4},{6,5},{7,6},{8,11},{9,8},{10,9... | collective-permute-start | bytes 491528 | tf_op jit(solution)/shard_map/ppermute | solution.py:542
  37.0 9.1 %copy-start.12 = (f32[1280]{0:T(1024)S(1)}, f32[1280]{0:T(1024)}, u32[]{:S(2)}) copy-start(f32[1280]{0:T(1024)} %param.29) | copy-start | bytes 15364
  37.0 11.7 %copy-start.14 = (f32[8,128]{1,0:T(8,128)S(1)}, f32[8,128]{1,0:T(8,128)}, u32[]{:S(2)}) copy-start(f32[8,128]{1,0:T(8,128)} %param.32) | copy-start | bytes 12292
  37.0 9.0 %collective-permute-start.3 = (bf16[64,1280]{1,0:T(8,128)(2,1)}, bf16[64,1280]{1,0:T(8,128)(2,1)}, u32[]{:S(2)}, u32[]{:S(2)}) collective-permute-start(bf16[64,1280]{1,0:T(8,128)(2,1)} %get-tuple-element.10), channel_id=1, source_target_pairs={{0,2},{1,3},{2,0},{3,1},{4,6},{5,7},{6,4},{7,5},{8,10},{9,11},{10,... | collective-permute-start | bytes 491528 | tf_op jit(solution)/shard_map/ppermute | solution.py:542
  47.4 7.4 %copy-start.10 = (bf16[64,1280]{1,0:T(8,128)(2,1)}, bf16[64,1280]{1,0:T(8,128)(2,1)S(1)}, u32[]{:S(2)}) copy-start(bf16[64,1280]{1,0:T(8,128)(2,1)S(1)} %get-tuple-element.7) | copy-start | bytes 491524
  47.4 8.6 %collective-permute-start.5 = (bf16[64,1280]{1,0:T(8,128)(2,1)S(1)}, bf16[64,1280]{1,0:T(8,128)(2,1)S(1)}, u32[]{:S(2)}, u32[]{:S(2)}) collective-permute-start(bf16[64,1280]{1,0:T(8,128)(2,1)S(1)} %get-tuple-element.7), channel_id=1, source_target_pairs={{0,1},{1,2},{2,3},{3,0},{4,5},{5,6},{6,7},{7,4},{8,9},{9,10},{10,1... | collective-permute-start | bytes 491528 | tf_op jit(solution)/shard_map/ppermute | solution.py:554
  54.8 6.0 %collective-permute-start.7 = (bf16[64,1280]{1,0:T(8,128)(2,1)S(1)}, bf16[64,1280]{1,0:T(8,128)(2,1)S(1)}, u32[]{:S(2)}, u32[]{:S(2)}) collective-permute-start(bf16[64,1280]{1,0:T(8,128)(2,1)S(1)} %get-tuple-element.7), channel_id=1, source_target_pairs={{0,3},{1,0},{2,1},{3,2},{4,7},{5,4},{6,5},{7,6},{8,11},{9,8},{10,9... | collective-permute-start | bytes 491528 | tf_op jit(solution)/shard_map/ppermute | solution.py:554
  54.8 5.5 %collective-permute-start.6 = (bf16[64,1280]{1,0:T(8,128)(2,1)S(1)}, bf16[64,1280]{1,0:T(8,128)(2,1)S(1)}, u32[]{:S(2)}, u32[]{:S(2)}) collective-permute-start(bf16[64,1280]{1,0:T(8,128)(2,1)S(1)} %get-tuple-element.7), channel_id=1, source_target_pairs={{0,2},{1,3},{2,0},{3,1},{4,6},{5,7},{6,4},{7,5},{8,10},{9,11},{10,... | collective-permute-start | bytes 491528 | tf_op jit(solution)/shard_map/ppermute | solution.py:554
  62.6 11.0 %collective-permute-start.9 = (bf16[256,2,256]{2,0,1:T(8,128)(2,1)S(1)}, bf16[256,2,256]{2,0,1:T(8,128)(2,1)S(1)}, u32[]{:S(2)}, u32[]{:S(2)}) collective-permute-start(bf16[256,2,256]{2,0,1:T(8,128)(2,1)S(1)} %bitcast.95), channel_id=1, source_target_pairs={{4,0},{8,4},{12,8},{16,12},{20,16},{24,20},{28,24},{5,1},{9,5},{13... | collective-permute-start | bytes 786440 | tf_op jit(solution)/shard_map/ppermute | solution.py:22
  63.9 15.4 %collective-permute-start.8 = (bf16[256,2,256]{2,0,1:T(8,128)(2,1)S(1)}, bf16[256,2,256]{2,0,1:T(8,128)(2,1)}, u32[]{:S(2)}, u32[]{:S(2)}) collective-permute-start(bf16[256,2,256]{2,0,1:T(8,128)(2,1)S(1)} %bitcast.96), channel_id=1, source_target_pairs={{0,4},{4,8},{8,12},{12,16},{16,20},{20,24},{24,28},{1,5},{5,9},{9,... | collective-permute-start | bytes 786440 | tf_op jit(solution)/shard_map/ppermute | solution.py:19
  69.5 2.9 copy-start.15
  69.6 11.7 %copy-start.4 = (f32[1024]{0:T(1024)S(1)}, f32[1024]{0:T(1024)}, u32[]{:S(2)}) copy-start(f32[1024]{0:T(1024)} %param.36) | copy-start | bytes 12292
  (12 other events, 16.9 us)
